TPU v7x, 256 devices: a whole 4x4x8 slice. The times are simulated.
256 devices in a mesh: seq: 32 (over x, y, z_hi), head: 8 (over z_lo, core).
Axes of the slice: x: 4, y: 4, z: 8 (z_hi: 2, z_lo: 4; z = z_hi * 4 + z_lo), core: 2. Of those that a mesh axis runs over, the one named last changes fastest.
Arguments:
- queries: bfloat16 [8192, 8192], P('seq', 'head'), may hold values from -6 to 6
- resp_kv: bfloat16 [8192, 2048], P('seq', 'head'), may hold values from -6 to 6
- prompt_cache: bfloat16 [16384, 2048], P(('seq', 'head')), may hold values from -6 to 6
- grad_out: bfloat16 [8192, 8192], P('seq', 'head'), may hold values from -96 to 96
- group_counts: int32 [8], replicated, may hold values from 1 to 16, 32 in all
- prompt_slot: int32 [8], replicated, may hold values from 0 to 7, each once
- slot_response: int32 [32], replicated, may hold values from 0 to 31, each once
- resp_len: int32 [32], P('seq'), may hold values from 1 to 256, as said below
- weight_code: int32 [32], P('seq'), may hold values from 1 to 16
Outputs:
- grad_queries: bfloat16 [8192, 8192], P('seq', 'head')
- grad_resp_kv: bfloat16 [8192, 2048], P('seq', 'head')
- grad_prompt_cache: bfloat16 [16384, 2048], P(('seq', 'head'))
Inputs may be any that keep to these rules, and one draw needn't show every extreme that they name: `group_counts`: they sum to 32, and the largest is 16. `prompt_slot`: each stored prompt belongs to exactly one group. `slot_response`: each response number stands in exactly one slot. `resp_len`: some slot holds a full response.
All inputs are finite; a program needn't handle non-finite values.
Results may differ from a plain program's by a relative error of at most 0.022.
Values may be sent and summed in bfloat16 or wider, within the bound.
A program may use at most 64 MiB of HBM per device.

v0:
```python
import math

import jax
import jax.numpy as jnp
from jax import lax
from jax.experimental import pallas as pl
from jax.experimental.pallas import tpu as pltpu
from jax.sharding import PartitionSpec as P

HD = 128
PLEN = 2048
RLEN = 256
HEADS = 8
PROMPTS = 8
RING = 16
CHUNK = PLEN // RING
UNITS = 4
UNIT = 16
BLOCK = 256
BLOCKS = PLEN // BLOCK
PER_BLOCK = BLOCK // CHUNK
ROWS = HEADS * RLEN
KEYS = PLEN + RLEN
WIDTH = 2 * HD
SCALE = HD**-0.5
LOG2E = math.log2(math.e)
MESH = pl.DeviceIdType.MESH
VMEM_LIMIT = 60 * 1024 * 1024
NN = (((1,), (0,)), ((), ()))
F32 = jnp.float32
BF16 = jnp.bfloat16


def around(index):
    return lax.rem(index + 2 * RING, RING)


def plus(plane, offset):
    return lax.rem(plane // 4 + offset // 4, 4) * 4 + lax.rem(plane + lax.rem(offset, 4), 4)


def minus(plane, offset):
    return lax.rem(plane // 4 + 4 - offset // 4, 4) * 4 + lax.rem(plane + 4 - lax.rem(offset, 4), 4)


def turn(place):
    return 5 * place % RING if isinstance(place, int) else lax.rem(5 * place, RING)


def unit_offset(column, u):
    return 4 * u + lax.rem(column + u, 4)


def column_step(i):
    return 8 + (i // 2) * (1 - 2 * lax.rem(i, 2))


def head_rows(j):
    return slice(j * RLEN, (j + 1) * RLEN)


def head_columns(j):
    return slice(j * HD, (j + 1) * HD)


def chunk_rows(step):
    return pl.ds(pl.multiple_of(step * CHUNK, CHUNK), CHUNK)


def fold(values, op):
    return op(values.reshape(values.shape[0] // 8, 8, values.shape[1]), axis=0)


def dot(a, b):
    return lax.dot_general(a, b, NN, preferred_element_type=F32)


def kernel(
    counts_ref,
    prompt_slot_ref,
    response_ref,
    len_ref,
    code_ref,
    q_ref,
    own_ref,
    cache_ref,
    go_ref,
    dq_ref,
    down_ref,
    back_ref,
    wanted,
    previous,
    last,
    q_in,
    go_in,
    own_in,
    rows_in,
    keys_in,
    values_in,
    staged,
    keys,
    values,
    q_rows,
    q_cols,
    cot_cols,
    cot_scaled_cols,
    cot_scaled_rows,
    scores,
    raw,
    top,
    delta,
    inverse,
    dq_cols,
    dv_sum,
    grads,
    terms,
    running,
    summed,
    sorted_sums,
    parts,
    final,
    own_grads,
    q_grads,
    in_sem,
    a_send,
    a_recv,
    b_send,
    b_recv,
    c_send,
    c_recv,
    rc_send,
    rc_recv,
    rb_send,
    rb_recv,
    ra_send,
    ra_recv,
):
    seq = lax.axis_index("seq")
    head = lax.axis_index("head")
    plane = seq // 2
    half = lax.rem(seq, 2)
    column = half * 8 + head

    def in_plane(other):
        return {"seq": 2 * other + half, "head": head}

    def in_column(other):
        return {"seq": 2 * plane + other // 8, "head": lax.rem(other, 8)}

    def remote(src, dst, send_sem, recv_sem, device):
        return pltpu.make_async_remote_copy(
            src_ref=src, dst_ref=dst, send_sem=send_sem, recv_sem=recv_sem, device_id=device, device_id_type=MESH
        )

    def all_at_once(buffer, sem):
        pltpu.make_async_copy(buffer.at[pl.ds(1, RING - 1)], buffer.at[pl.ds(1, RING - 1)], sem).wait()

    loads = [
        pltpu.make_async_copy(q_ref, q_in, in_sem.at[0]),
        pltpu.make_async_copy(go_ref, go_in, in_sem.at[1]),
        pltpu.make_async_copy(own_ref, own_in, in_sem.at[2]),
    ]
    for load in loads:
        load.start()

    barrier = pltpu.get_barrier_semaphore()

    def greet(step, carry):
        pl.semaphore_signal(barrier, inc=1, device_id=in_column(around(column + step)), device_id_type=MESH)
        pl.semaphore_signal(barrier, inc=1, device_id=in_plane(plus(plane, step)), device_id_type=MESH)
        return carry

    lax.fori_loop(1, RING, greet, 0)
    pl.semaphore_wait(barrier, 2 * (RING - 1))

    stays = lax.rem(column, 4) == 0

    def unit_copy(u):
        return remote(
            cache_ref.at[pl.ds(u * UNIT, UNIT)],
            rows_in.at[u],
            a_send.at[u],
            a_recv.at[u],
            in_plane(plus(plane, unit_offset(column, u))),
        )

    for u in range(1, UNITS):
        unit_copy(u).start()

    @pl.when(jnp.logical_not(stays))
    def _():
        unit_copy(0).start()

    @pl.when(stays)
    def _():
        pltpu.make_async_copy(cache_ref.at[pl.ds(0, UNIT)], rows_in.at[0], a_recv.at[0]).start()

    by_source = (keys_in, values_in)

    def column_copy(part, step):
        target = around(column + step)
        at = pl.ds(pl.multiple_of(lax.rem(target, 8) * WIDTH + part * HD, HD), HD)
        return remote(
            rows_in.at[:, :, at], by_source[part].at[column], b_send.at[part], b_recv.at[part], in_column(target)
        )

    def send_heads(part):
        def send(i, carry):
            column_copy(part, column_step(i)).start()
            return carry

        lax.fori_loop(1, RING, send, 0)
        by_source[part][column] = rows_in[:, :, pl.ds(pl.multiple_of(head * WIDTH + part * HD, HD), HD)]

    gathered = (keys, values)

    def chunk_copy(part, step):
        return remote(
            staged.at[part, step],
            gathered[part].at[chunk_rows(step)],
            c_send.at[part],
            c_recv.at[part, step],
            in_plane(plus(plane, turn(step))),
        )

    def send_chunks(part):
        def take(step):
            prompt = wanted[step]
            units = []
            for odd in range(2):
                across = lax.rem(lax.div(plane, 4) + 4 - lax.div(prompt, 2), 4)
                along = lax.rem(plane + 4 - 2 * lax.rem(prompt, 2) - odd, 4)
                first = lax.rem(along + 4 - across, 4)
                for i in range(4):
                    units.append(by_source[part][4 * i + first, across])
            return jnp.concatenate(units, axis=0)

        all_at_once(by_source[part], b_recv.at[part])
        for step in range(1, RING):
            staged[part, step] = take(step)
            chunk_copy(part, step).start()
        gathered[part][:CHUNK] = take(0)

    ends = []
    for i in range(PROMPTS):
        ends.append(counts_ref[i] + (ends[-1] if ends else 0))
    prompts = []
    for step in range(RING):
        response = response_ref[2 * plus(plane, turn(step)) + half]
        group = jnp.int32(0)
        for end in ends[:-1]:
            group = group + (end <= response).astype(jnp.int32)
        prompts.append(prompt_slot_ref[group])
        wanted[step] = prompts[-1]
    for step in range(RING):
        found = jnp.int32(RING)
        for other in range(step):
            found = jnp.where(prompts[other] == prompts[step], other, found)
        previous[step] = found
    for prompt in range(PROMPTS):
        found = jnp.int32(RING)
        for step in range(RING):
            found = jnp.where(prompts[step] == prompt, step, found)
        last[prompt] = found

    for load in loads:
        load.wait()
    position = lax.broadcasted_iota(jnp.int32, (RLEN, HD), 0)
    factor = jnp.where(position < len_ref[0], code_ref[0].astype(F32) / 8.0, 0.0)
    for j in range(HEADS):
        query = q_in[:, head_columns(j)]
        q_rows[head_rows(j)] = query
        q_cols[:, head_rows(j)] = jnp.transpose(query)
        cotangent = go_in[:, head_columns(j)].astype(F32) * factor
        cot_cols[:, head_rows(j)] = jnp.transpose(cotangent).astype(BF16)
    keys[PLEN:] = own_in[:, :HD]
    values[PLEN:] = own_in[:, HD:]
    running[RING] = jnp.zeros((CHUNK, HD), F32)
    dq_cols[...] = jnp.zeros_like(dq_cols)

    def block_rows(b):
        return pl.ds(pl.multiple_of(b * BLOCK, BLOCK), BLOCK)

    def score(b, own):
        block = keys[block_rows(b)]
        for j in range(HEADS):
            at = head_rows(j)
            part = dot(block, q_cols[:, at])
            if own:
                key_at = lax.broadcasted_iota(jnp.int32, (BLOCK, RLEN), 0)
                seen_from = lax.broadcasted_iota(jnp.int32, (BLOCK, RLEN), 1)
                part = jnp.where(key_at <= seen_from, part, -1e30)
            scores[b, :, at] = part
            high = fold(part, jnp.max)
            top[:, at] = high if own else jnp.maximum(top[:, at], high)

    for u in range(UNITS):
        unit_copy(u).wait_recv()
    send_heads(0)
    send_heads(1)
    score(BLOCKS, True)
    send_chunks(0)
    send_chunks(1)

    def arrive(part, b):
        def one(i, carry):
            step = b * PER_BLOCK + i

            @pl.when(step > 0)
            def _():
                chunk_copy(part, step).wait_recv()

            return carry

        lax.fori_loop(0, PER_BLOCK, one, 0)

    def score_block(b, carry):
        arrive(0, b)
        score(b, False)
        return carry

    lax.fori_loop(0, BLOCKS, score_block, 0)

    def return_copy(part, step):
        return remote(
            grads.at[part, step],
            terms.at[part, step],
            rc_send.at[part],
            rc_recv.at[part],
            in_plane(minus(plane, turn(step))),
        )

    def send_back(part, b, block):
        for i in range(PER_BLOCK):
            grads[part, b * PER_BLOCK + i] = block[i * CHUNK : (i + 1) * CHUNK]

        def one(i, carry):
            step = b * PER_BLOCK + i

            @pl.when(step > 0)
            def _():
                return_copy(part, step).start()

            return carry

        lax.fori_loop(0, PER_BLOCK, one, 0)

    def pair_rows(p):
        return slice(2 * p * RLEN, 2 * (p + 1) * RLEN)

    def pair_grads(b, p):
        return dot(raw[b, :, pair_rows(p)], cot_scaled_rows[pair_rows(p)])

    for p in range(HEADS // 2):
        heads = (2 * p, 2 * p + 1)
        highest = [jnp.max(top[:, head_rows(j)], axis=0, keepdims=True) for j in heads]

        def weigh(b, totals):
            sums = []
            for j, high, total in zip(heads, highest, totals):
                at = head_rows(j)
                weights = jnp.exp2((scores[b, :, at] - high) * (SCALE * LOG2E))
                raw[b, :, at] = weights.astype(BF16)
                sums.append(total + fold(weights, jnp.sum))
            if p == 1:
                dv_sum[b] = pair_grads(b, 0)
            elif p > 1:
                dv_sum[b] += pair_grads(b, p - 1)
            return tuple(sums)

        totals = lax.fori_loop(0, BLOCKS + 1, weigh, (jnp.zeros((8, RLEN), F32),) * 2)
        for j, total in zip(heads, totals):
            at = head_rows(j)
            over = 1.0 / jnp.sum(total, axis=0, keepdims=True)
            inverse[:, at] = jnp.broadcast_to(over, (8, RLEN))
            scaled = cot_cols[:, at].astype(F32) * over
            cot_scaled_cols[:, at] = scaled.astype(BF16)
            cot_scaled_rows[at] = jnp.transpose(scaled).astype(BF16)

    def value_grads(b):
        return (dv_sum[b] + pair_grads(b, HEADS // 2 - 1)).astype(BF16)

    def value_block(b, carry):
        send_back(1, b, value_grads(b))
        return carry

    lax.fori_loop(0, BLOCKS, value_block, 0)

    def look(b, first):
        block = values[block_rows(b)]
        for j in range(HEADS):
            at = head_rows(j)
            grad = dot(block, cot_scaled_cols[:, at])
            scores[b, :, at] = grad
            term = fold(grad * raw[b, :, at].astype(F32), jnp.sum)
            delta[:, at] = term if first else delta[:, at] + term

    def look_block(b, carry):
        arrive(1, b)
        look(b, False)
        return carry

    look(BLOCKS, True)
    lax.fori_loop(0, BLOCKS, look_block, 0)
    for j in range(HEADS):
        at = head_rows(j)
        delta[:, at] = jnp.sum(delta[:, at], axis=0, keepdims=True) * inverse[:, at]

    def key_part(b):
        turned = jnp.transpose(keys[block_rows(b)])
        for j in range(HEADS):
            at = head_rows(j)
            weights = raw[b, :, at].astype(F32)
            shift = delta[0:1, at]
            change = (weights * (scores[b, :, at] - shift)).astype(BF16)
            raw[b, :, at] = change
            dq_cols[:, at] += dot(turned, change)
        return (dot(raw[b], q_rows[...]) * SCALE).astype(BF16)

    def key_block(b, carry):
        send_back(0, b, key_part(b))
        return carry

    lax.fori_loop(0, 4, key_block, 0)

    def return_column(part, step):
        target = around(column + step)
        return remote(
            sorted_sums.at[part, target],
            parts.at[part, column],
            rb_send.at[part],
            rb_recv.at[part],
            in_column(target),
        )

    def add_up(part):
        all_at_once(grads.at[part], rc_recv.at[part])
        terms[part, 0] = grads[part, 0]

        def add(step, carry):
            running[step] = running[previous[step]] + terms[part, step].astype(F32)
            return carry

        lax.fori_loop(0, RING, add, 0)

        def close(prompt, carry):
            summed[prompt] = running[last[prompt]].astype(BF16)
            return carry

        lax.fori_loop(0, PROMPTS, close, 0)

        def sort(target):
            for u in range(UNITS):
                source = minus(plane, unit_offset(target, u))
                unit = lax.rem(source, 2) * 4 + target // 4
                sorted_sums[part, target, u * UNIT : (u + 1) * UNIT] = summed[
                    source // 2, pl.ds(pl.multiple_of(unit * UNIT, UNIT), UNIT)
                ]

        def send(i, carry):
            step = column_step(i)
            sort(around(column + step))
            return_column(part, step).start()
            return carry

        lax.fori_loop(1, RING, send, 0)
        sort(column)
        parts[part, column] = sorted_sums[part, column]

    def return_unit(part, u):
        return remote(
            final.at[part, pl.ds(u * UNIT, UNIT)],
            back_ref.at[part, pl.ds(u * UNIT, UNIT)],
            ra_send.at[part, u],
            ra_recv.at[part, u],
            in_plane(minus(plane, unit_offset(column, u))),
        )

    def return_stay(part):
        return pltpu.make_async_copy(
            final.at[part, pl.ds(0, UNIT)], back_ref.at[part, pl.ds(0, UNIT)], ra_recv.at[part, 0]
        )

    def return_rows(part):
        all_at_once(parts.at[part], rb_recv.at[part])
        for h in range(8):
            both = parts[part, h].astype(F32) + parts[part, 8 + h].astype(F32)
            final[part, :, head_columns(h)] = both.astype(BF16)
        for u in range(1, UNITS):
            return_unit(part, u).start()

        @pl.when(jnp.logical_not(stays))
        def _():
            return_unit(part, 0).start()

        @pl.when(stays)
        def _():
            return_stay(part).start()

    add_up(1)
    lax.fori_loop(4, BLOCKS, key_block, 0)

    own_grads[:, HD:] = value_grads(BLOCKS)
    own_grads[:, :HD] = key_part(BLOCKS)
    own_out = pltpu.make_async_copy(own_grads, down_ref, in_sem.at[2])
    own_out.start()
    return_rows(1)
    for j in range(HEADS):
        q_grads[:, head_columns(j)] = (jnp.transpose(dq_cols[:, head_rows(j)]) * SCALE).astype(BF16)
    q_out = pltpu.make_async_copy(q_grads, dq_ref, in_sem.at[0])
    q_out.start()
    add_up(0)
    return_rows(0)

    own_out.wait()
    q_out.wait()
    for part in range(2):
        all_at_once(by_source[part], b_send.at[part])
        all_at_once(staged.at[part], c_send.at[part])
        all_at_once(grads.at[part], rc_send.at[part])
        all_at_once(parts.at[part], rb_send.at[part])
        for u in range(UNITS):
            return_unit(part, u).wait_recv()
        for u in range(1, UNITS):
            return_unit(part, u).wait_send()
    for u in range(1, UNITS):
        unit_copy(u).wait_send()

    @pl.when(jnp.logical_not(stays))
    def _():
        unit_copy(0).wait_send()
        return_unit(0, 0).wait_send()
        return_unit(1, 0).wait_send()


def finish_kernel(dq_ref, down_ref, back_ref, dq_out, down_out, dcache_out, dq, down, back, total, get_sems, put_sems):
    gets = [
        pltpu.make_async_copy(back_ref, back, get_sems.at[0]),
        pltpu.make_async_copy(dq_ref, dq, get_sems.at[1]),
        pltpu.make_async_copy(down_ref, down, get_sems.at[2]),
    ]
    puts = [
        pltpu.make_async_copy(total, dcache_out, put_sems.at[0]),
        pltpu.make_async_copy(dq, dq_out, put_sems.at[1]),
        pltpu.make_async_copy(down, down_out, put_sems.at[2]),
    ]
    for get in gets:
        get.start()
    gets[0].wait()
    for h in range(8):
        for part in range(2):
            total[:, h * WIDTH + part * HD : h * WIDTH + (part + 1) * HD] = back[part, :, head_columns(h)]
    puts[0].start()
    for get, put in zip(gets[1:], puts[1:]):
        get.wait()
        put.start()
    for put in puts:
        put.wait()


def local(
    queries, resp_kv, prompt_cache, grad_out, group_counts, prompt_slot, slot_response, resp_len, weight_code
):
    smem = pl.BlockSpec(memory_space=pltpu.SMEM)
    hbm = pl.BlockSpec(memory_space=pltpu.HBM)
    scratch = [
        pltpu.SMEM((RING,), jnp.int32),
        pltpu.SMEM((RING,), jnp.int32),
        pltpu.SMEM((PROMPTS,), jnp.int32),
        pltpu.VMEM((RLEN, HEADS * HD), BF16),
        pltpu.VMEM((RLEN, HEADS * HD), BF16),
        pltpu.VMEM((RLEN, WIDTH), BF16),
        pltpu.VMEM((UNITS, UNIT, 8 * WIDTH), BF16),
        pltpu.VMEM((RING, UNITS, UNIT, HD), BF16),
        pltpu.VMEM((RING, UNITS, UNIT, HD), BF16),
        pltpu.VMEM((2, RING, CHUNK, HD), BF16),
        pltpu.VMEM((KEYS, HD), BF16),
        pltpu.VMEM((KEYS, HD), BF16),
        pltpu.VMEM((ROWS, HD), BF16),
        pltpu.VMEM((HD, ROWS), BF16),
        pltpu.VMEM((HD, ROWS), BF16),
        pltpu.VMEM((HD, ROWS), BF16),
        pltpu.VMEM((ROWS, HD), BF16),
        pltpu.VMEM((BLOCKS + 1, BLOCK, ROWS), F32),
        pltpu.VMEM((BLOCKS + 1, BLOCK, ROWS), BF16),
        pltpu.VMEM((8, ROWS), F32),
        pltpu.VMEM((8, ROWS), F32),
        pltpu.VMEM((8, ROWS), F32),
        pltpu.VMEM((HD, ROWS), F32),
        pltpu.VMEM((BLOCKS + 1, BLOCK, HD), F32),
        pltpu.VMEM((2, RING, CHUNK, HD), BF16),
        pltpu.VMEM((2, RING, CHUNK, HD), BF16),
        pltpu.VMEM((RING + 1, CHUNK, HD), F32),
        pltpu.VMEM((PROMPTS, CHUNK, HD), BF16),
        pltpu.VMEM((2, RING, UNITS * UNIT, HD), BF16),
        pltpu.VMEM((2, RING, UNITS * UNIT, HD), BF16),
        pltpu.VMEM((2, UNITS * UNIT, 8 * HD), BF16),
        pltpu.VMEM((RLEN, WIDTH), BF16),
        pltpu.VMEM((RLEN, HEADS * HD), BF16),
        pltpu.SemaphoreType.DMA((3,)),
        pltpu.SemaphoreType.DMA((UNITS,)),
        pltpu.SemaphoreType.DMA((UNITS,)),
        pltpu.SemaphoreType.DMA((2,)),
        pltpu.SemaphoreType.DMA((2,)),
        pltpu.SemaphoreType.DMA((2,)),
        pltpu.SemaphoreType.DMA((2, RING)),
        pltpu.SemaphoreType.DMA((2,)),
        pltpu.SemaphoreType.DMA((2,)),
        pltpu.SemaphoreType.DMA((2,)),
        pltpu.SemaphoreType.DMA((2,)),
        pltpu.SemaphoreType.DMA((2, UNITS)),
        pltpu.SemaphoreType.DMA((2, UNITS)),
    ]
    products = 5 * ROWS * KEYS * HD
    dq, down, back = pl.pallas_call(
        kernel,
        out_shape=[
            jax.ShapeDtypeStruct(queries.shape, BF16),
            jax.ShapeDtypeStruct(resp_kv.shape, BF16),
            jax.ShapeDtypeStruct((2, UNITS * UNIT, 8 * HD), BF16),
        ],
        in_specs=[smem] * 5 + [hbm] * 4,
        out_specs=[hbm] * 3,
        scratch_shapes=scratch,
        compiler_params=pltpu.CompilerParams(
            collective_id=0, has_side_effects=True, vmem_limit_bytes=VMEM_LIMIT
        ),
        cost_estimate=pl.CostEstimate(flops=2 * products, bytes_accessed=3 << 20, transcendentals=ROWS * KEYS),
    )(
        group_counts,
        prompt_slot,
        slot_response,
        resp_len,
        weight_code,
        queries,
        resp_kv,
        prompt_cache,
        grad_out,
    )
    return pl.pallas_call(
        finish_kernel,
        out_shape=[
            jax.ShapeDtypeStruct(queries.shape, BF16),
            jax.ShapeDtypeStruct(resp_kv.shape, BF16),
            jax.ShapeDtypeStruct(prompt_cache.shape, BF16),
        ],
        in_specs=[hbm] * 3,
        out_specs=[hbm] * 3,
        scratch_shapes=[
            pltpu.VMEM(queries.shape, BF16),
            pltpu.VMEM(resp_kv.shape, BF16),
            pltpu.VMEM((2, UNITS * UNIT, 8 * HD), BF16),
            pltpu.VMEM(prompt_cache.shape, BF16),
            pltpu.SemaphoreType.DMA((3,)),
            pltpu.SemaphoreType.DMA((3,)),
        ],
        compiler_params=pltpu.CompilerParams(vmem_limit_bytes=VMEM_LIMIT),
    )(dq, down, back)


def solution(mesh):
    placed = (
        P("seq", "head"),
        P("seq", "head"),
        P(("seq", "head"), None),
        P("seq", "head"),
        P(),
        P(),
        P(),
        P("seq"),
        P("seq"),
    )
    return jax.shard_map(
        local,
        mesh=mesh,
        in_specs=placed,
        out_specs=(P("seq", "head"), P("seq", "head"), P(("seq", "head"), None)),
        check_vma=False,
    )
```

profile of v0, /device:TPU:1, one launch (start us, length us, event | category | flops | bytes accessed | tf_op | source)
XLA Modules:
  0.0 80.6 jit_solution(13920926364444766807)
XLA Ops:
  1.9 76.7 %shard_map.112 = (bf16[256,1024]{1,0:T(8,128)(2,1)}, bf16[256,256]{1,0:T(8,128)(2,1)}, bf16[2,64,1024]{2,1,0:T(8,128)(2,1)}) custom-call(s32[8]{0:T(128)} %counts_ref.1, s32[8]{0:T(128)} %prompt_slot_ref.1, s32[32]{0:T(128)} %response_ref.1, s32[1]{0:T(128)S(6)} %copy.12.len_ref, s32[1]{0:T(128)S(6)} %copy.13.code_ref, bf16[256,1024]{1,0:T(8,128)(2,1)} %q_ref.1, ...), custom_call_target="tpu_custom_call" | custom-call | flops 6039797760 | bytes 3145728 | tf_op jit(solution)/shard_map/pallas_call | solution.py:615
  78.6 2.0 %shard_map.113 = (bf16[256,1024]{1,0:T(8,128)(2,1)}, bf16[256,256]{1,0:T(8,128)(2,1)}, bf16[64,2048]{1,0:T(8,128)(2,1)}) custom-call(bf16[256,1024]{1,0:T(8,128)(2,1)} %get-tuple-element.6.dq_ref, bf16[256,256]{1,0:T(8,128)(2,1)} %get-tuple-element.7.down_ref, bf16[2,64,1024]{2,1,0:T(8,128)(2,1)} %get-tuple-element.8.back_ref), custom_call_target="tpu_custom_call" | custom-call | tf_op jit(solution)/shard_map/pallas_call | solution.py:640
where the time goes:
time: 81.3 us; the launch traced here: 80.6 us
  Pallas kernels  78.7 us (97%)
  between operations  1.93 us (2%)
    pallas_call x1, Pallas kernels, local(): pl.pallas_call(kernel, out_shape=[jax.ShapeDtypeStruct(queries.shape, BF1...  76.7 us
    pallas_call x1, Pallas kernels, local(): pl.pallas_call(finish_kernel, out_shape=[jax.ShapeDtypeStruct(queries.sha...  2 us

commit v1 on v0

--- a/solution.py
+++ b/solution.py
@@ -110,7 +110,7 @@
     top,
     delta,
     inverse,
-    dq_cols,
+    turned,
     dv_sum,
     grads,
     terms,
@@ -276,7 +276,6 @@
     keys[PLEN:] = own_in[:, :HD]
     values[PLEN:] = own_in[:, HD:]
     running[RING] = jnp.zeros((CHUNK, HD), F32)
-    dq_cols[...] = jnp.zeros_like(dq_cols)
 
     def block_rows(b):
         return pl.ds(pl.multiple_of(b * BLOCK, BLOCK), BLOCK)
@@ -407,21 +406,19 @@
         delta[:, at] = jnp.sum(delta[:, at], axis=0, keepdims=True) * inverse[:, at]
 
     def key_part(b):
-        turned = jnp.transpose(keys[block_rows(b)])
         for j in range(HEADS):
             at = head_rows(j)
             weights = raw[b, :, at].astype(F32)
             shift = delta[0:1, at]
             change = (weights * (scores[b, :, at] - shift)).astype(BF16)
             raw[b, :, at] = change
-            dq_cols[:, at] += dot(turned, change)
         return (dot(raw[b], q_rows[...]) * SCALE).astype(BF16)
 
     def key_block(b, carry):
         send_back(0, b, key_part(b))
         return carry
 
-    lax.fori_loop(0, 4, key_block, 0)
+    lax.fori_loop(0, BLOCKS, key_block, 0)
 
     def return_column(part, step):
         target = around(column + step)
@@ -498,18 +495,24 @@
             return_stay(part).start()
 
     add_up(1)
-    lax.fori_loop(4, BLOCKS, key_block, 0)
 
     own_grads[:, HD:] = value_grads(BLOCKS)
     own_grads[:, :HD] = key_part(BLOCKS)
     own_out = pltpu.make_async_copy(own_grads, down_ref, in_sem.at[2])
     own_out.start()
-    return_rows(1)
-    for j in range(HEADS):
-        q_grads[:, head_columns(j)] = (jnp.transpose(dq_cols[:, head_rows(j)]) * SCALE).astype(BF16)
+    turned[...] = jnp.transpose(keys[...])
+
+    def query_grads(first, end):
+        for j in range(first, end):
+            grad = dot(turned[...], raw[:, :, head_rows(j)].reshape(KEYS, RLEN))
+            q_grads[:, head_columns(j)] = (jnp.transpose(grad) * SCALE).astype(BF16)
+
+    query_grads(0, 2)
+    add_up(0)
+    query_grads(2, HEADS)
     q_out = pltpu.make_async_copy(q_grads, dq_ref, in_sem.at[0])
     q_out.start()
-    add_up(0)
+    return_rows(1)
     return_rows(0)
 
     own_out.wait()
@@ -586,7 +589,7 @@
         pltpu.VMEM((8, ROWS), F32),
         pltpu.VMEM((8, ROWS), F32),
         pltpu.VMEM((8, ROWS), F32),
-        pltpu.VMEM((HD, ROWS), F32),
+        pltpu.VMEM((HD, KEYS), BF16),
         pltpu.VMEM((BLOCKS + 1, BLOCK, HD), F32),
         pltpu.VMEM((2, RING, CHUNK, HD), BF16),
         pltpu.VMEM((2, RING, CHUNK, HD), BF16),

time: 81.3 us -> 78.2 us (0.962)
  Pallas kernels: 78.7 us -> 76.1 us
    pallas_call x1, Pallas kernels: 76.7 us -> 74.1 us  [local(): pl.pallas_call(kernel, out_shape=[jax.ShapeDtypeStruct(queries.shape, BF1...]
where the time goes in v1:
time: 78.2 us; the launch traced here: 78 us
  Pallas kernels  76.1 us (97%)
  between operations  1.93 us (2%)
    pallas_call x1, Pallas kernels, local(): pl.pallas_call(kernel, out_shape=[jax.ShapeDtypeStruct(queries.shape, BF1...  74.1 us
    pallas_call x1, Pallas kernels, local(): pl.pallas_call(finish_kernel, out_shape=[jax.ShapeDtypeStruct(queries.sha...  2 us

profile of v1, /device:TPU:1, one launch (start us, length us, event | category | flops | bytes accessed | tf_op | source)
XLA Modules:
  0.0 78.0 jit_solution(7231722057991429493)
XLA Ops:
  1.9 74.1 %shard_map.112 = (bf16[256,1024]{1,0:T(8,128)(2,1)}, bf16[256,256]{1,0:T(8,128)(2,1)}, bf16[2,64,1024]{2,1,0:T(8,128)(2,1)}) custom-call(s32[8]{0:T(128)} %counts_ref.1, s32[8]{0:T(128)} %prompt_slot_ref.1, s32[32]{0:T(128)} %response_ref.1, s32[1]{0:T(128)S(6)} %copy.12.len_ref, s32[1]{0:T(128)S(6)} %copy.13.code_ref, bf16[256,1024]{1,0:T(8,128)(2,1)} %q_ref.1, ...), custom_call_target="tpu_custom_call" | custom-call | flops 6039797760 | bytes 3145728 | tf_op jit(solution)/shard_map/pallas_call | solution.py:618
  76.0 2.0 %shard_map.113 = (bf16[256,1024]{1,0:T(8,128)(2,1)}, bf16[256,256]{1,0:T(8,128)(2,1)}, bf16[64,2048]{1,0:T(8,128)(2,1)}) custom-call(bf16[256,1024]{1,0:T(8,128)(2,1)} %get-tuple-element.6.dq_ref, bf16[256,256]{1,0:T(8,128)(2,1)} %get-tuple-element.7.down_ref, bf16[2,64,1024]{2,1,0:T(8,128)(2,1)} %get-tuple-element.8.back_ref), custom_call_target="tpu_custom_call" | custom-call | tf_op jit(solution)/shard_map/pallas_call | solution.py:643

commit v2 on v1

--- a/solution.py
+++ b/solution.py
@@ -116,9 +116,6 @@
     terms,
     running,
     summed,
-    sorted_sums,
-    parts,
-    final,
     own_grads,
     q_grads,
     in_sem,
@@ -132,8 +129,7 @@
     rc_recv,
     rb_send,
     rb_recv,
-    ra_send,
-    ra_recv,
+    stay_sem,
 ):
     seq = lax.axis_index("seq")
     head = lax.axis_index("head")
@@ -420,14 +416,22 @@
 
     lax.fori_loop(0, BLOCKS, key_block, 0)
 
-    def return_column(part, step):
-        target = around(column + step)
+    def home_copy(part, target, u):
+        source = minus(plane, unit_offset(target, u))
+        unit = lax.rem(source, 2) * 4 + target // 4
         return remote(
-            sorted_sums.at[part, target],
-            parts.at[part, column],
+            summed.at[part, source // 2, unit],
+            back_ref.at[part, 4 * column + u],
             rb_send.at[part],
             rb_recv.at[part],
-            in_column(target),
+            {"seq": 2 * source + target // 8, "head": lax.rem(target, 8)},
+        )
+
+    def home_stay(part):
+        return pltpu.make_async_copy(
+            summed.at[part, plane // 2, lax.rem(plane, 2) * 4 + column // 4],
+            back_ref.at[part, 4 * column],
+            stay_sem.at[part],
         )
 
     def add_up(part):
@@ -441,58 +445,38 @@
         lax.fori_loop(0, RING, add, 0)
 
         def close(prompt, carry):
-            summed[prompt] = running[last[prompt]].astype(BF16)
+            summed[part, prompt] = running[last[prompt]].astype(BF16).reshape(CHUNK // UNIT, UNIT, HD)
             return carry
 
         lax.fori_loop(0, PROMPTS, close, 0)
 
-        def sort(target):
+        def send(i, carry):
+            target = around(column + column_step(i))
             for u in range(UNITS):
-                source = minus(plane, unit_offset(target, u))
-                unit = lax.rem(source, 2) * 4 + target // 4
-                sorted_sums[part, target, u * UNIT : (u + 1) * UNIT] = summed[
-                    source // 2, pl.ds(pl.multiple_of(unit * UNIT, UNIT), UNIT)
-                ]
-
-        def send(i, carry):
-            step = column_step(i)
-            sort(around(column + step))
-            return_column(part, step).start()
+                home_copy(part, target, u).start()
             return carry
 
         lax.fori_loop(1, RING, send, 0)
-        sort(column)
-        parts[part, column] = sorted_sums[part, column]
-
-    def return_unit(part, u):
-        return remote(
-            final.at[part, pl.ds(u * UNIT, UNIT)],
-            back_ref.at[part, pl.ds(u * UNIT, UNIT)],
-            ra_send.at[part, u],
-            ra_recv.at[part, u],
-            in_plane(minus(plane, unit_offset(column, u))),
-        )
-
-    def return_stay(part):
-        return pltpu.make_async_copy(
-            final.at[part, pl.ds(0, UNIT)], back_ref.at[part, pl.ds(0, UNIT)], ra_recv.at[part, 0]
-        )
-
-    def return_rows(part):
-        all_at_once(parts.at[part], rb_recv.at[part])
-        for h in range(8):
-            both = parts[part, h].astype(F32) + parts[part, 8 + h].astype(F32)
-            final[part, :, head_columns(h)] = both.astype(BF16)
         for u in range(1, UNITS):
-            return_unit(part, u).start()
+            home_copy(part, column, u).start()
 
         @pl.when(jnp.logical_not(stays))
         def _():
-            return_unit(part, 0).start()
+            home_copy(part, column, 0).start()
 
         @pl.when(stays)
         def _():
-            return_stay(part).start()
+            home_stay(part).start()
+
+    def home_wait(part, sem):
+        @pl.when(jnp.logical_not(stays))
+        def _():
+            pltpu.make_async_copy(back_ref.at[part], back_ref.at[part], sem).wait()
+
+        @pl.when(stays)
+        def _():
+            rest = back_ref.at[part, pl.ds(1, RING * UNITS - 1)]
+            pltpu.make_async_copy(rest, rest, sem).wait()
 
     add_up(1)
 
@@ -512,28 +496,27 @@
     query_grads(2, HEADS)
     q_out = pltpu.make_async_copy(q_grads, dq_ref, in_sem.at[0])
     q_out.start()
-    return_rows(1)
-    return_rows(0)
 
     own_out.wait()
     q_out.wait()
+    for u in range(1, UNITS):
+        unit_copy(u).wait_send()
+
+    @pl.when(jnp.logical_not(stays))
+    def _():
+        unit_copy(0).wait_send()
+
     for part in range(2):
         all_at_once(by_source[part], b_send.at[part])
         all_at_once(staged.at[part], c_send.at[part])
         all_at_once(grads.at[part], rc_send.at[part])
-        all_at_once(parts.at[part], rb_send.at[part])
-        for u in range(UNITS):
-            return_unit(part, u).wait_recv()
-        for u in range(1, UNITS):
-            return_unit(part, u).wait_send()
-    for u in range(1, UNITS):
-        unit_copy(u).wait_send()
-
-    @pl.when(jnp.logical_not(stays))
-    def _():
-        unit_copy(0).wait_send()
-        return_unit(0, 0).wait_send()
-        return_unit(1, 0).wait_send()
+    for part in (1, 0):
+        home_wait(part, rb_send.at[part])
+        home_wait(part, rb_recv.at[part])
+
+        @pl.when(stays)
+        def _():
+            home_stay(part).wait()
 
 
 def finish_kernel(dq_ref, down_ref, back_ref, dq_out, down_out, dcache_out, dq, down, back, total, get_sems, put_sems):
@@ -552,7 +535,10 @@
     gets[0].wait()
     for h in range(8):
         for part in range(2):
-            total[:, h * WIDTH + part * HD : h * WIDTH + (part + 1) * HD] = back[part, :, head_columns(h)]
+            first = back[part, UNITS * h : UNITS * (h + 1)].astype(F32)
+            second = back[part, UNITS * (8 + h) : UNITS * (9 + h)].astype(F32)
+            both = (first + second).astype(BF16).reshape(UNITS * UNIT, HD)
+            total[:, h * WIDTH + part * HD : h * WIDTH + (part + 1) * HD] = both
     puts[0].start()
     for get, put in zip(gets[1:], puts[1:]):
         get.wait()
@@ -594,10 +580,7 @@
         pltpu.VMEM((2, RING, CHUNK, HD), BF16),
         pltpu.VMEM((2, RING, CHUNK, HD), BF16),
         pltpu.VMEM((RING + 1, CHUNK, HD), F32),
-        pltpu.VMEM((PROMPTS, CHUNK, HD), BF16),
-        pltpu.VMEM((2, RING, UNITS * UNIT, HD), BF16),
-        pltpu.VMEM((2, RING, UNITS * UNIT, HD), BF16),
-        pltpu.VMEM((2, UNITS * UNIT, 8 * HD), BF16),
+        pltpu.VMEM((2, PROMPTS, CHUNK // UNIT, UNIT, HD), BF16),
         pltpu.VMEM((RLEN, WIDTH), BF16),
         pltpu.VMEM((RLEN, HEADS * HD), BF16),
         pltpu.SemaphoreType.DMA((3,)),
@@ -611,8 +594,7 @@
         pltpu.SemaphoreType.DMA((2,)),
         pltpu.SemaphoreType.DMA((2,)),
         pltpu.SemaphoreType.DMA((2,)),
-        pltpu.SemaphoreType.DMA((2, UNITS)),
-        pltpu.SemaphoreType.DMA((2, UNITS)),
+        pltpu.SemaphoreType.DMA((2,)),
     ]
     products = 5 * ROWS * KEYS * HD
     dq, down, back = pl.pallas_call(
@@ -620,7 +602,7 @@
         out_shape=[
             jax.ShapeDtypeStruct(queries.shape, BF16),
             jax.ShapeDtypeStruct(resp_kv.shape, BF16),
-            jax.ShapeDtypeStruct((2, UNITS * UNIT, 8 * HD), BF16),
+            jax.ShapeDtypeStruct((2, RING * UNITS, UNIT, HD), BF16),
         ],
         in_specs=[smem] * 5 + [hbm] * 4,
         out_specs=[hbm] * 3,
@@ -652,7 +634,7 @@
         scratch_shapes=[
             pltpu.VMEM(queries.shape, BF16),
             pltpu.VMEM(resp_kv.shape, BF16),
-            pltpu.VMEM((2, UNITS * UNIT, 8 * HD), BF16),
+            pltpu.VMEM((2, RING * UNITS, UNIT, HD), BF16),
             pltpu.VMEM(prompt_cache.shape, BF16),
             pltpu.SemaphoreType.DMA((3,)),
             pltpu.SemaphoreType.DMA((3,)),

time: 78.2 us -> 77.1 us (0.986)
  Pallas kernels: 76.1 us -> 75 us
    pallas_call x1, Pallas kernels: 74.1 us -> 72.9 us  [local(): pl.pallas_call(kernel, out_shape=[jax.ShapeDtypeStruct(queries.shape, BF1...]
where the time goes in v2:
time: 77.1 us; the launch traced here: 76.9 us
  Pallas kernels  75 us (97%)
  between operations  1.93 us (3%)
    pallas_call x1, Pallas kernels, local(): pl.pallas_call(kernel, out_shape=[jax.ShapeDtypeStruct(queries.shape, BF1...  72.9 us
    pallas_call x1, Pallas kernels, local(): pl.pallas_call(finish_kernel, out_shape=[jax.ShapeDtypeStruct(queries.sha...  2.08 us

profile of v2, /device:TPU:1, one launch (start us, length us, event | category | flops | bytes accessed | tf_op | source)
XLA Modules:
  0.0 76.9 jit_solution(802025425822839550)
XLA Ops:
  1.9 72.9 %shard_map.112 = (bf16[256,1024]{1,0:T(8,128)(2,1)}, bf16[256,256]{1,0:T(8,128)(2,1)}, bf16[2,64,16,128]{3,2,1,0:T(8,128)(2,1)}) custom-call(s32[8]{0:T(128)} %counts_ref.1, s32[8]{0:T(128)} %prompt_slot_ref.1, s32[32]{0:T(128)} %response_ref.1, s32[1]{0:T(128)S(6)} %copy.12.len_ref, s32[1]{0:T(128)S(6)} %copy.13.code_ref, bf16[256,1024]{1,0:T(8,128)(2,1)} %q_ref.1, ...), custom_call_target="tpu_custom_call" | custom-call | flops 6039797760 | bytes 3145728 | tf_op jit(solution)/shard_map/pallas_call | solution.py:600
  74.8 2.1 %shard_map.113 = (bf16[256,1024]{1,0:T(8,128)(2,1)}, bf16[256,256]{1,0:T(8,128)(2,1)}, bf16[64,2048]{1,0:T(8,128)(2,1)}) custom-call(bf16[256,1024]{1,0:T(8,128)(2,1)} %get-tuple-element.6.dq_ref, bf16[256,256]{1,0:T(8,128)(2,1)} %get-tuple-element.7.down_ref, bf16[2,64,16,128]{3,2,1,0:T(8,128)(2,1)} %get-tuple-element.8.back_ref), custom_call_target="tpu_custom_call" | custom-call | tf_op jit(solution)/shard_map/pallas_call | solution.py:625

commit v3 on v2

--- a/solution.py
+++ b/solution.py
@@ -35,16 +35,24 @@
     return lax.rem(index + 2 * RING, RING)
 
 
+def div(a, b):
+    return a // b if isinstance(a, int) else lax.div(a, b)
+
+
+def rem(a, b):
+    return a % b if isinstance(a, int) else lax.rem(a, b)
+
+
 def plus(plane, offset):
-    return lax.rem(plane // 4 + offset // 4, 4) * 4 + lax.rem(plane + lax.rem(offset, 4), 4)
+    return 4 * rem(div(plane, 4) + div(offset, 4), 4) + rem(plane + rem(offset, 4), 4)
 
 
 def minus(plane, offset):
-    return lax.rem(plane // 4 + 4 - offset // 4, 4) * 4 + lax.rem(plane + 4 - lax.rem(offset, 4), 4)
+    return 4 * rem(div(plane, 4) + 4 - div(offset, 4), 4) + rem(plane + 4 - rem(offset, 4), 4)
 
 
 def turn(place):
-    return 5 * place % RING if isinstance(place, int) else lax.rem(5 * place, RING)
+    return rem(5 * place, RING)
 
 
 def unit_offset(column, u):
@@ -52,7 +60,7 @@
 
 
 def column_step(i):
-    return 8 + (i // 2) * (1 - 2 * lax.rem(i, 2))
+    return 8 + div(i, 2) * (1 - 2 * rem(i, 2))
 
 
 def head_rows(j):
@@ -88,7 +96,8 @@
     dq_ref,
     down_ref,
     back_ref,
-    wanted,
+    across,
+    first,
     previous,
     last,
     q_in,
@@ -133,7 +142,7 @@
 ):
     seq = lax.axis_index("seq")
     head = lax.axis_index("head")
-    plane = seq // 2
+    plane = div(seq, 2)
     half = lax.rem(seq, 2)
     column = half * 8 + head
 
@@ -141,7 +150,7 @@
         return {"seq": 2 * other + half, "head": head}
 
     def in_column(other):
-        return {"seq": 2 * plane + other // 8, "head": lax.rem(other, 8)}
+        return {"seq": 2 * plane + div(other, 8), "head": lax.rem(other, 8)}
 
     def remote(src, dst, send_sem, recv_sem, device):
         return pltpu.make_async_remote_copy(
@@ -160,16 +169,31 @@
         load.start()
 
     barrier = pltpu.get_barrier_semaphore()
-
-    def greet(step, carry):
-        pl.semaphore_signal(barrier, inc=1, device_id=in_column(around(column + step)), device_id_type=MESH)
-        pl.semaphore_signal(barrier, inc=1, device_id=in_plane(plus(plane, step)), device_id_type=MESH)
+    stays = rem(column, 4) == 0
+
+    def greet(device):
+        pl.semaphore_signal(barrier, inc=1, device_id=device, device_id_type=MESH)
+
+    def greet_column(step, carry):
+        greet(in_column(around(column + step)))
         return carry
 
-    lax.fori_loop(1, RING, greet, 0)
-    pl.semaphore_wait(barrier, 2 * (RING - 1))
-
-    stays = lax.rem(column, 4) == 0
+    def greet_unit(u):
+        greet(in_plane(plus(plane, unit_offset(column, u))))
+        greet(in_plane(minus(plane, unit_offset(column, u))))
+
+    lax.fori_loop(1, RING, greet_column, 0)
+    for u in range(1, UNITS):
+        greet_unit(u)
+
+    @pl.when(stays)
+    def _():
+        pl.semaphore_wait(barrier, RING - 1 + 2 * (UNITS - 1))
+
+    @pl.when(jnp.logical_not(stays))
+    def _():
+        greet_unit(0)
+        pl.semaphore_wait(barrier, RING - 1 + 2 * UNITS)
 
     def unit_copy(u):
         return remote(
@@ -220,15 +244,8 @@
         )
 
     def send_chunks(part):
-        def take(step):
-            prompt = wanted[step]
-            units = []
-            for odd in range(2):
-                across = lax.rem(lax.div(plane, 4) + 4 - lax.div(prompt, 2), 4)
-                along = lax.rem(plane + 4 - 2 * lax.rem(prompt, 2) - odd, 4)
-                first = lax.rem(along + 4 - across, 4)
-                for i in range(4):
-                    units.append(by_source[part][4 * i + first, across])
+        def take(place):
+            units = [by_source[part][4 * i + first[odd, place], across[place]] for odd in range(2) for i in range(4)]
             return jnp.concatenate(units, axis=0)
 
         all_at_once(by_source[part], b_recv.at[part])
@@ -246,8 +263,12 @@
         group = jnp.int32(0)
         for end in ends[:-1]:
             group = group + (end <= response).astype(jnp.int32)
-        prompts.append(prompt_slot_ref[group])
-        wanted[step] = prompts[-1]
+        prompt = prompt_slot_ref[group]
+        prompts.append(prompt)
+        way = rem(div(plane, 4) + 4 - div(prompt, 2), 4)
+        across[step] = way
+        for odd in range(2):
+            first[odd, step] = rem(plane + 8 - 2 * rem(prompt, 2) - odd - way, 4)
     for step in range(RING):
         found = jnp.int32(RING)
         for other in range(step):
@@ -417,19 +438,20 @@
     lax.fori_loop(0, BLOCKS, key_block, 0)
 
     def home_copy(part, target, u):
-        source = minus(plane, unit_offset(target, u))
-        unit = lax.rem(source, 2) * 4 + target // 4
+        x = rem(div(plane, 4) + 4 - u, 4)
+        y = rem(plane + 20 - target - u, 4)
+        source = 4 * x + y
         return remote(
-            summed.at[part, source // 2, unit],
+            summed.at[part, 4 * source + div(target, 4)],
             back_ref.at[part, 4 * column + u],
             rb_send.at[part],
             rb_recv.at[part],
-            {"seq": 2 * source + target // 8, "head": lax.rem(target, 8)},
+            {"seq": 2 * source + div(target, 8), "head": rem(target, 8)},
         )
 
     def home_stay(part):
         return pltpu.make_async_copy(
-            summed.at[part, plane // 2, lax.rem(plane, 2) * 4 + column // 4],
+            summed.at[part, 4 * plane + div(column, 4)],
             back_ref.at[part, 4 * column],
             stay_sem.at[part],
         )
@@ -445,7 +467,8 @@
         lax.fori_loop(0, RING, add, 0)
 
         def close(prompt, carry):
-            summed[part, prompt] = running[last[prompt]].astype(BF16).reshape(CHUNK // UNIT, UNIT, HD)
+            units = running[last[prompt]].astype(BF16).reshape(CHUNK // UNIT, UNIT, HD)
+            summed[part, pl.ds(prompt * (CHUNK // UNIT), CHUNK // UNIT)] = units
             return carry
 
         lax.fori_loop(0, PROMPTS, close, 0)
@@ -554,6 +577,7 @@
     hbm = pl.BlockSpec(memory_space=pltpu.HBM)
     scratch = [
         pltpu.SMEM((RING,), jnp.int32),
+        pltpu.SMEM((2, RING), jnp.int32),
         pltpu.SMEM((RING,), jnp.int32),
         pltpu.SMEM((PROMPTS,), jnp.int32),
         pltpu.VMEM((RLEN, HEADS * HD), BF16),
@@ -580,7 +604,7 @@
         pltpu.VMEM((2, RING, CHUNK, HD), BF16),
         pltpu.VMEM((2, RING, CHUNK, HD), BF16),
         pltpu.VMEM((RING + 1, CHUNK, HD), F32),
-        pltpu.VMEM((2, PROMPTS, CHUNK // UNIT, UNIT, HD), BF16),
+        pltpu.VMEM((2, RING * UNITS, UNIT, HD), BF16),
         pltpu.VMEM((RLEN, WIDTH), BF16),
         pltpu.VMEM((RLEN, HEADS * HD), BF16),
         pltpu.SemaphoreType.DMA((3,)),

time: 77.1 us -> 77.2 us (level)
  no operation moved by 1% of the time
where the time goes in v3:
time: 77.2 us; the launch traced here: 77 us
  Pallas kernels  75.1 us (97%)
  between operations  1.93 us (2%)
    pallas_call x1, Pallas kernels, local(): pl.pallas_call(kernel, out_shape=[jax.ShapeDtypeStruct(queries.shape, BF1...  73 us
    pallas_call x1, Pallas kernels, local(): pl.pallas_call(finish_kernel, out_shape=[jax.ShapeDtypeStruct(queries.sha...  2.08 us

profile of v3, /device:TPU:1, one launch (start us, length us, event | category | flops | bytes accessed | tf_op | source)
XLA Modules:
  0.0 77.0 jit_solution(13585864090944955065)
XLA Ops:
  1.9 73.0 %shard_map.112 = (bf16[256,1024]{1,0:T(8,128)(2,1)}, bf16[256,256]{1,0:T(8,128)(2,1)}, bf16[2,64,16,128]{3,2,1,0:T(8,128)(2,1)}) custom-call(s32[8]{0:T(128)} %counts_ref.1, s32[8]{0:T(128)} %prompt_slot_ref.1, s32[32]{0:T(128)} %response_ref.1, s32[1]{0:T(128)S(6)} %copy.12.len_ref, s32[1]{0:T(128)S(6)} %copy.13.code_ref, bf16[256,1024]{1,0:T(8,128)(2,1)} %q_ref.1, ...), custom_call_target="tpu_custom_call" | custom-call | flops 6039797760 | bytes 3145728 | tf_op jit(solution)/shard_map/pallas_call | solution.py:624
  75.0 2.1 %shard_map.113 = (bf16[256,1024]{1,0:T(8,128)(2,1)}, bf16[256,256]{1,0:T(8,128)(2,1)}, bf16[64,2048]{1,0:T(8,128)(2,1)}) custom-call(bf16[256,1024]{1,0:T(8,128)(2,1)} %get-tuple-element.6.dq_ref, bf16[256,256]{1,0:T(8,128)(2,1)} %get-tuple-element.7.down_ref, bf16[2,64,16,128]{3,2,1,0:T(8,128)(2,1)} %get-tuple-element.8.back_ref), custom_call_target="tpu_custom_call" | custom-call | tf_op jit(solution)/shard_map/pallas_call | solution.py:649

commit v4 on v3

--- a/solution.py
+++ b/solution.py
@@ -384,7 +384,7 @@
                 dv_sum[b] += pair_grads(b, p - 1)
             return tuple(sums)
 
-        totals = lax.fori_loop(0, BLOCKS + 1, weigh, (jnp.zeros((8, RLEN), F32),) * 2)
+        totals = lax.fori_loop(0, BLOCKS + 1, weigh, (jnp.zeros((8, RLEN), F32),) * 2, unroll=3)
         for j, total in zip(heads, totals):
             at = head_rows(j)
             over = 1.0 / jnp.sum(total, axis=0, keepdims=True)
@@ -411,13 +411,12 @@
             term = fold(grad * raw[b, :, at].astype(F32), jnp.sum)
             delta[:, at] = term if first else delta[:, at] + term
 
-    def look_block(b, carry):
+    look(BLOCKS, True)
+    for b in range(0, BLOCKS, 2):
         arrive(1, b)
+        arrive(1, b + 1)
         look(b, False)
-        return carry
-
-    look(BLOCKS, True)
-    lax.fori_loop(0, BLOCKS, look_block, 0)
+        look(b + 1, False)
     for j in range(HEADS):
         at = head_rows(j)
         delta[:, at] = jnp.sum(delta[:, at], axis=0, keepdims=True) * inverse[:, at]
@@ -431,11 +430,10 @@
             raw[b, :, at] = change
         return (dot(raw[b], q_rows[...]) * SCALE).astype(BF16)
 
-    def key_block(b, carry):
-        send_back(0, b, key_part(b))
-        return carry
-
-    lax.fori_loop(0, BLOCKS, key_block, 0)
+    for b in range(0, BLOCKS, 2):
+        key_grads = [key_part(b), key_part(b + 1)]
+        send_back(0, b, key_grads[0])
+        send_back(0, b + 1, key_grads[1])
 
     def home_copy(part, target, u):
         x = rem(div(plane, 4) + 4 - u, 4)

time: 77.2 us -> 74.3 us (0.962)
  Pallas kernels: 75.1 us -> 72.2 us
    pallas_call x1, Pallas kernels: 73 us -> 70.1 us  [local(): pl.pallas_call(kernel, out_shape=[jax.ShapeDtypeStruct(queries.shape, BF1...]
where the time goes in v4:
time: 74.3 us; the launch traced here: 74.2 us
  Pallas kernels  72.2 us (97%)
  between operations  1.93 us (3%)
    pallas_call x1, Pallas kernels, local(): pl.pallas_call(kernel, out_shape=[jax.ShapeDtypeStruct(queries.shape, BF1...  70.1 us
    pallas_call x1, Pallas kernels, local(): pl.pallas_call(finish_kernel, out_shape=[jax.ShapeDtypeStruct(queries.sha...  2.08 us

profile of v4, /device:TPU:1, one launch (start us, length us, event | category | flops | bytes accessed | tf_op | source)
XLA Modules:
  0.0 74.2 jit_solution(2765402146539329384)
XLA Ops:
  1.9 70.1 %shard_map.112 = (bf16[256,1024]{1,0:T(8,128)(2,1)}, bf16[256,256]{1,0:T(8,128)(2,1)}, bf16[2,64,16,128]{3,2,1,0:T(8,128)(2,1)}) custom-call(s32[8]{0:T(128)} %counts_ref.1, s32[8]{0:T(128)} %prompt_slot_ref.1, s32[32]{0:T(128)} %response_ref.1, s32[1]{0:T(128)S(6)} %copy.12.len_ref, s32[1]{0:T(128)S(6)} %copy.13.code_ref, bf16[256,1024]{1,0:T(8,128)(2,1)} %q_ref.1, ...), custom_call_target="tpu_custom_call" | custom-call | flops 6039797760 | bytes 3145728 | tf_op jit(solution)/shard_map/pallas_call | solution.py:622
  72.1 2.1 %shard_map.113 = (bf16[256,1024]{1,0:T(8,128)(2,1)}, bf16[256,256]{1,0:T(8,128)(2,1)}, bf16[64,2048]{1,0:T(8,128)(2,1)}) custom-call(bf16[256,1024]{1,0:T(8,128)(2,1)} %get-tuple-element.6.dq_ref, bf16[256,256]{1,0:T(8,128)(2,1)} %get-tuple-element.7.down_ref, bf16[2,64,16,128]{3,2,1,0:T(8,128)(2,1)} %get-tuple-element.8.back_ref), custom_call_target="tpu_custom_call" | custom-call | tf_op jit(solution)/shard_map/pallas_call | solution.py:647

commit v5 on v4

--- a/solution.py
+++ b/solution.py
@@ -330,12 +330,11 @@
 
         lax.fori_loop(0, PER_BLOCK, one, 0)
 
-    def score_block(b, carry):
+    for b in range(0, BLOCKS, 2):
         arrive(0, b)
+        arrive(0, b + 1)
         score(b, False)
-        return carry
-
-    lax.fori_loop(0, BLOCKS, score_block, 0)
+        score(b + 1, False)
 
     def return_copy(part, step):
         return remote(
@@ -384,7 +383,9 @@
                 dv_sum[b] += pair_grads(b, p - 1)
             return tuple(sums)
 
-        totals = lax.fori_loop(0, BLOCKS + 1, weigh, (jnp.zeros((8, RLEN), F32),) * 2, unroll=3)
+        totals = (jnp.zeros((8, RLEN), F32),) * 2
+        for b in range(BLOCKS + 1):
+            totals = weigh(b, totals)
         for j, total in zip(heads, totals):
             at = head_rows(j)
             over = 1.0 / jnp.sum(total, axis=0, keepdims=True)
@@ -396,11 +397,10 @@
     def value_grads(b):
         return (dv_sum[b] + pair_grads(b, HEADS // 2 - 1)).astype(BF16)
 
-    def value_block(b, carry):
-        send_back(1, b, value_grads(b))
-        return carry
-
-    lax.fori_loop(0, BLOCKS, value_block, 0)
+    for b in range(0, BLOCKS, 2):
+        block_grads = [value_grads(b), value_grads(b + 1)]
+        send_back(1, b, block_grads[0])
+        send_back(1, b + 1, block_grads[1])
 
     def look(b, first):
         block = values[block_rows(b)]

time: 74.3 us -> 73.5 us (0.989)
  Pallas kernels: 72.2 us -> 71.2 us
    pallas_call x1, Pallas kernels: 70.1 us -> 69.1 us  [local(): pl.pallas_call(kernel, out_shape=[jax.ShapeDtypeStruct(queries.shape, BF1...]
where the time goes in v5:
time: 73.5 us; the launch traced here: 73.3 us
  Pallas kernels  71.2 us (97%)
  between operations  2.09 us (3%)
    pallas_call x1, Pallas kernels, local(): pl.pallas_call(kernel, out_shape=[jax.ShapeDtypeStruct(queries.shape, BF1...  69.1 us
    pallas_call x1, Pallas kernels, local(): pl.pallas_call(finish_kernel, out_shape=[jax.ShapeDtypeStruct(queries.sha...  2.08 us

profile of v5, /device:TPU:1, one launch (start us, length us, event | category | flops | bytes accessed | tf_op | source)
XLA Modules:
  0.0 73.3 jit_solution(13901183953901613650)
XLA Ops:
  1.9 69.1 %shard_map.112 = (bf16[256,1024]{1,0:T(8,128)(2,1)}, bf16[256,256]{1,0:T(8,128)(2,1)}, bf16[2,64,16,128]{3,2,1,0:T(8,128)(2,1)}) custom-call(s32[8]{0:T(128)} %counts_ref.1, s32[8]{0:T(128)} %prompt_slot_ref.1, s32[32]{0:T(128)} %response_ref.1, s32[1]{0:T(128)S(6)} %copy.12.len_ref, s32[1]{0:T(128)S(6)} %copy.13.code_ref, bf16[256,1024]{1,0:T(8,128)(2,1)} %q_ref.1, ...), custom_call_target="tpu_custom_call" | custom-call | flops 6039797760 | bytes 3145728 | tf_op jit(solution)/shard_map/pallas_call | solution.py:622
  71.1 2.1 %shard_map.113 = (bf16[256,1024]{1,0:T(8,128)(2,1)}, bf16[256,256]{1,0:T(8,128)(2,1)}, bf16[64,2048]{1,0:T(8,128)(2,1)}) custom-call(bf16[256,1024]{1,0:T(8,128)(2,1)} %get-tuple-element.6.dq_ref, bf16[256,256]{1,0:T(8,128)(2,1)} %get-tuple-element.7.down_ref, bf16[2,64,16,128]{3,2,1,0:T(8,128)(2,1)} %get-tuple-element.8.back_ref), custom_call_target="tpu_custom_call" | custom-call | tf_op jit(solution)/shard_map/pallas_call | solution.py:647

commit v6 on v5

--- a/solution.py
+++ b/solution.py
@@ -412,11 +412,11 @@
             delta[:, at] = term if first else delta[:, at] + term
 
     look(BLOCKS, True)
-    for b in range(0, BLOCKS, 2):
-        arrive(1, b)
-        arrive(1, b + 1)
-        look(b, False)
-        look(b + 1, False)
+    for b in range(0, BLOCKS, 4):
+        for i in range(4):
+            arrive(1, b + i)
+        for i in range(4):
+            look(b + i, False)
     for j in range(HEADS):
         at = head_rows(j)
         delta[:, at] = jnp.sum(delta[:, at], axis=0, keepdims=True) * inverse[:, at]
@@ -462,14 +462,14 @@
             running[step] = running[previous[step]] + terms[part, step].astype(F32)
             return carry
 
-        lax.fori_loop(0, RING, add, 0)
+        lax.fori_loop(0, RING, add, 0, unroll=4)
 
         def close(prompt, carry):
             units = running[last[prompt]].astype(BF16).reshape(CHUNK // UNIT, UNIT, HD)
             summed[part, pl.ds(prompt * (CHUNK // UNIT), CHUNK // UNIT)] = units
             return carry
 
-        lax.fori_loop(0, PROMPTS, close, 0)
+        lax.fori_loop(0, PROMPTS, close, 0, unroll=4)
 
         def send(i, carry):
             target = around(column + column_step(i))

time: 73.5 us -> 73.1 us (level)
  no operation moved by 1% of the time
where the time goes in v6:
time: 73.1 us; the launch traced here: 72.9 us
  Pallas kernels  70.8 us (97%)
  between operations  2.09 us (3%)
    pallas_call x1, Pallas kernels, local(): pl.pallas_call(kernel, out_shape=[jax.ShapeDtypeStruct(queries.shape, BF1...  68.7 us
    pallas_call x1, Pallas kernels, local(): pl.pallas_call(finish_kernel, out_shape=[jax.ShapeDtypeStruct(queries.sha...  2.08 us

profile of v6, /device:TPU:1, one launch (start us, length us, event | category | flops | bytes accessed | tf_op | source)
XLA Modules:
  0.0 72.9 jit_solution(771725314626094627)
XLA Ops:
  1.9 68.7 %shard_map.112 = (bf16[256,1024]{1,0:T(8,128)(2,1)}, bf16[256,256]{1,0:T(8,128)(2,1)}, bf16[2,64,16,128]{3,2,1,0:T(8,128)(2,1)}) custom-call(s32[8]{0:T(128)} %counts_ref.1, s32[8]{0:T(128)} %prompt_slot_ref.1, s32[32]{0:T(128)} %response_ref.1, s32[1]{0:T(128)S(6)} %copy.12.len_ref, s32[1]{0:T(128)S(6)} %copy.13.code_ref, bf16[256,1024]{1,0:T(8,128)(2,1)} %q_ref.1, ...), custom_call_target="tpu_custom_call" | custom-call | flops 6039797760 | bytes 3145728 | tf_op jit(solution)/shard_map/pallas_call | solution.py:622
  70.7 2.1 %shard_map.113 = (bf16[256,1024]{1,0:T(8,128)(2,1)}, bf16[256,256]{1,0:T(8,128)(2,1)}, bf16[64,2048]{1,0:T(8,128)(2,1)}) custom-call(bf16[256,1024]{1,0:T(8,128)(2,1)} %get-tuple-element.6.dq_ref, bf16[256,256]{1,0:T(8,128)(2,1)} %get-tuple-element.7.down_ref, bf16[2,64,16,128]{3,2,1,0:T(8,128)(2,1)} %get-tuple-element.8.back_ref), custom_call_target="tpu_custom_call" | custom-call | tf_op jit(solution)/shard_map/pallas_call | solution.py:647
